TPU v7x, 32 devices: a whole 2x2x4 slice. The times are simulated.
32 devices in a mesh: parts: 2 (over x), tp: 8 (over z, y), ep: 2 (over core).
Axes of the slice: x: 2, y: 2, z: 4, core: 2. Of those that a mesh axis runs over, the one named last changes fastest.
Arguments:
- tokens: bfloat16 [2048, 6144], P(('parts', 'tp')), parts along dimension 0, may hold values from -6 to 6
- expert_ids: int32 [2048, 2], P(('parts', 'tp')), parts along dimension 0, may hold values from 0 to 7, all different within a row; in each aligned block of 128 rows (0 to 127, 128 to 255, ...) at most 36 rows name the same one
- route_weight: float32 [2048, 2], P(('parts', 'tp')), parts along dimension 0, may hold values from 0.2 to 1
- w_gate: bfloat16 [2, 6144, 8192], P('ep', None, 'tp'), may hold values from -0.078125 to 0.078125
- w_up: bfloat16 [2, 6144, 8192], P('ep', None, 'tp'), may hold values from -0.078125 to 0.078125
- w_down: bfloat16 [2, 8192, 6144], P('ep', 'tp'), may hold values from -0.0625 to 0.0625
- round_bits: int32 [2, 8, 288], P('ep', 'tp'), may hold values from 0 to 1073741823
Outputs:
- mixed: bfloat16 [2048, 6144], P(('parts', 'tp'), 'ep'), parts along dimension 0
There are 2 independent parts, one for each index of `parts`. A program takes and returns all parts, laid end to end along the dimension named above; an argument that names none is the same for every part. Nothing has to cross between parts.
Inputs may be any that keep to these rules, and one draw needn't show every extreme that they name: `expert_ids`: A token's 2 ids differ. In each aligned block of 128 tokens (the tokens of one index of tp) no expert is named by more than 36 tokens, and in some blocks some expert is named by exactly 36.
All inputs are finite; a program needn't handle non-finite values.
Results may differ from a plain program's by a relative error of at most 0.015.
Values may be sent and summed in bfloat16 or wider, within the bound.
A program may use at most 128 MiB of HBM per device.

v0:
```python
import jax
import jax.numpy as jnp
from jax import lax
from jax.sharding import PartitionSpec as P

SLOT = 36


def dither(partial_value, row_bits):
    columns = jnp.arange(partial_value.shape[1], dtype=jnp.int32)
    mixed_bits = (row_bits[:, None] + 40503 * columns[None, :]) % 65536
    factor = 0.5 + mixed_bits.astype(jnp.float32) / 65536.0
    return (partial_value * factor).astype(jnp.bfloat16)


def shards(tokens, expert_ids, route_weight, w_gate, w_up, w_down, round_bits):
    expert = lax.axis_index("ep")
    slot_index = jnp.arange(SLOT, dtype=jnp.int32)
    chosen = expert_ids == expert
    targeted = jnp.any(chosen, axis=1)
    ordinal = jnp.cumsum(targeted.astype(jnp.int32)) - 1
    placing = (targeted[None, :] & (ordinal[None, :] == slot_index[:, None])).astype(jnp.bfloat16)
    route_share = jnp.sum(jnp.where(chosen, route_weight, 0.0), axis=1)
    outgoing = jnp.dot(placing, tokens, preferred_element_type=jnp.float32).astype(jnp.bfloat16)
    gate_w = w_gate[0]
    up_w = w_up[0]
    down_w = w_down[0]
    row_noise = round_bits[0, 0]
    row_block = lax.all_gather(outgoing, "tp", axis=0, tiled=True)
    gate_act = jnp.dot(row_block, gate_w, preferred_element_type=jnp.float32)
    up_act = jnp.dot(row_block, up_w, preferred_element_type=jnp.float32)
    hidden = (jax.nn.silu(gate_act) * up_act).astype(jnp.bfloat16)
    partial_value = jnp.dot(hidden, down_w, preferred_element_type=jnp.float32)
    rounded = dither(partial_value, row_noise)
    returned = (
        lax.psum_scatter(rounded, "tp", scatter_dimension=0, tiled=True)
        .astype(jnp.float32)
        .astype(jnp.bfloat16)
    )
    gathered_back = jnp.einsum("st,sd->td", placing, returned, preferred_element_type=jnp.float32)
    weighted = route_share[:, None] * gathered_back
    output = lax.psum_scatter(weighted.astype(jnp.bfloat16), "ep", scatter_dimension=1, tiled=True)
    return output


def solution(mesh):
    return jax.shard_map(
        shards,
        mesh=mesh,
        in_specs=(
            P(("parts", "tp"), None),
            P(("parts", "tp"), None),
            P(("parts", "tp"), None),
            P("ep", None, "tp"),
            P("ep", None, "tp"),
            P("ep", "tp", None),
            P("ep", "tp", None),
        ),
        out_specs=P(("parts", "tp"), "ep"),
        check_vma=False,
    )
```

profile of v0, /device:TPU:1, one launch (start us, length us, event | category | flops | bytes accessed | tf_op | source)
XLA Modules:
  0.0 229.1 jit_solution(4863310366803658418)
XLA Ops:
  6.5 0.0 copy-start
  6.5 0.8 fusion.37
  7.4 0.1 copy.10
  7.5 0.2 reduce-window.8
  7.7 0.1 add_reduce_fusion
  7.8 0.2 copy-done
  8.0 1.1 fusion.18
  9.1 0.0 all-gather.3.cloned.1.call-update
  9.1 0.0 reduce-scatter.4.cloned.1.call-start
  9.2 0.7 reduce.1
  9.9 70.8 %all-gather.3.cloned.1.call-done = bf16[8,36,6144]{2,1,0:T(8,128)(2,1)} async-done(((bf16[1,36,6144]{2,1,0:T(8,128)(2,1)}), bf16[8,36,6144]{2,1,0:T(8,128)(2,1)}) %all-gather.3.cloned.1.call-update) | async-done | bytes 3538960 | tf_op jit(solution)/shard_map/all_gather | solution.py:29
  80.7 4.7 %reshape.42 = bf16[288,6144]{1,0:T(8,128)(2,1)} reshape(bf16[8,36,6144]{2,1,0:T(8,128)(2,1)} %all-gather.3.cloned.1.call-done) | data formatting | bytes 7077888
  85.4 7.9 %fusion.5 = f32[288,1024]{1,0:T(8,128)S(1)} fusion(bf16[288,6144]{1,0:T(8,128)(2,1)} %reshape.42, bf16[1,6144,1024]{2,1,0:T(8,128)(2,1)} %param.10), kind=kOutput, calls=%fused_computation.7 | convolution fusion | flops 3623878656 | bytes 17301504 | tf_op jit(solution)/shard_map/dot_general | solution.py:30
  93.3 21.1 %fusion.10 = bf16[288,6144]{1,0:T(8,128)(2,1)} fusion(bf16[1,1024,6144]{2,1,0:T(8,128)(2,1)} %param.12, s32[6144]{0:T(1024)S(1)} %iota_multiply_fusion, s32[288]{0:T(512)S(1)} %reduce.1, bf16[288,6144]{1,0:T(8,128)(2,1)} %reshape.42, bf16[1,6144,1024]{2,1,0:T(8,128)(2,1)} %param.11, f32[288,1024]{1,0:T(8,128)S(1)} %fusion.5), kind=kOutput, calls=%fused_computation.12 | convolution fusion | flops 7279607808 | bytes 33449088 | tf_op jit(solution)/shard_map/dot_general | solution.py:33
  114.4 77.6 %fusion = bf16[40,6144]{1,0:T(8,128)(2,1)S(1)} fusion(bf16[288,6144]{1,0:T(8,128)(2,1)} %fusion.10), kind=kCustom, calls=%all-reduce-scatter | all-reduce-scatter fusion | flops 1966081 | bytes 4030976
  191.9 0.1 slice
  192.0 4.1 %collective-permute-start = (bf16[28,6144]{1,0:T(8,128)(2,1)S(1)}, bf16[28,6144]{1,0:T(8,128)(2,1)S(1)}, u32[]{:S(2)}, u32[]{:S(2)}) collective-permute-start(bf16[28,6144]{1,0:T(8,128)(2,1)S(1)} %slice), channel_id=1, source_target_pairs={{0,2},{2,4},{4,6},{6,8},{8,10},{10,12},{12,14},{1,3},{3,5},{5,7},{... | collective-permute-start | bytes 1032200
  196.2 0.0 copy-done.3
  196.2 0.6 dynamic-slice.4
  197.5 3.4 %collective-permute-done = bf16[28,6144]{1,0:T(8,128)(2,1)S(1)} collective-permute-done((bf16[28,6144]{1,0:T(8,128)(2,1)S(1)}, bf16[28,6144]{1,0:T(8,128)(2,1)S(1)}, u32[]{:S(2)}, u32[]{:S(2)}) %collective-permute-start) | collective-permute-done | bytes 344096
  200.9 0.7 concatenate
  201.6 1.8 fusion.13
  203.4 0.0 reduce-scatter.4.cloned.1.call-update
  203.4 18.8 %reduce-scatter.4.cloned.1.call-done = bf16[128,3072]{1,0:T(8,128)(2,1)} async-done(((bf16[128,6144]{1,0:T(8,128)(2,1)}), bf16[128,3072]{1,0:T(8,128)(2,1)}) %reduce-scatter.4.cloned.1.call-update) | async-done | bytes 786448 | tf_op jit(solution)/shard_map/reduce_scatter | solution.py:42
  (9 shorter events, 0.0 us)
Async XLA Ops:
  6.5 1.4 copy-start
  6.5 74.1 %all-gather.3.cloned.1.call-start = ((), (), s32[]{:S(2)}) async-start(), calls=%async_computation.2 | async-start | bytes 4423680 | tf_op jit(solution)/shard_map/all_gather | solution.py:29
  9.1 213.1 %reduce-scatter.4.cloned.1.call-start = ((), (), s32[]{:S(2)}) async-start(), calls=%async_computation.1 | async-start | bytes 2359296 | tf_op jit(solution)/shard_map/reduce_scatter | solution.py:42
  114.4 81.8 %copy-start.3 = (u32[32]{0:T(128)S(1)}, u32[32]{0:T(128)}, u32[]{:S(2)}) copy-start(u32[32]{0:T(128)} %constant.45) | copy-start | bytes 388
  114.4 83.1 %copy-start.1 = (s32[128,2]{0,1:T(2,128)S(1)}, s32[128,2]{0,1:T(2,128)}, u32[]{:S(2)}) copy-start(s32[128,2]{0,1:T(2,128)} %param.8) | copy-start | bytes 3076
  114.4 83.1 %copy-start.2 = (f32[128,2]{0,1:T(2,128)S(1)}, f32[128,2]{0,1:T(2,128)}, u32[]{:S(2)}) copy-start(f32[128,2]{0,1:T(2,128)} %param.9) | copy-start | bytes 3076
  192.0 8.8 %collective-permute-start = (bf16[28,6144]{1,0:T(8,128)(2,1)S(1)}, bf16[28,6144]{1,0:T(8,128)(2,1)S(1)}, u32[]{:S(2)}, u32[]{:S(2)}) collective-permute-start(bf16[28,6144]{1,0:T(8,128)(2,1)S(1)} %slice), channel_id=1, source_target_pairs={{0,2},{2,4},{4,6},{6,8},{8,10},{10,12},{12,14},{1,3},{3,5},{5,7},{... | collective-permute-start | bytes 1032200
Sparse Core Ops, SparseCore 0:
  9.5 71.0 all-gather.2
  203.5 18.6 reduce-scatter.3
where the time goes:
time: 230 us; the launch traced here: 229 us
  waiting for transfers between devices  93.1 us (40%)
  blocking collectives  77.6 us (34%)
  matrix products  31.9 us (14%)
  between operations  14.1 us (6%)
  local copies, waits for them, and re-layouts  6.46 us (3%)
  starting transfers between devices  4.17 us (2%)
    unnamed x1, blocking collectives  77.6 us
    all_gather x1, waiting for transfers between devices, shards(): row_block = lax.all_gather(outgoing, 'tp', axis=0, tiled=True)  70.8 us
    dot_general x1, matrix products, shards(): partial_value = jnp.dot(hidden, down_w, preferred_element_type=jnp.float32)  21.1 us
    reduce_scatter x1, waiting for transfers between devices, shards(): lax.psum_scatter(weighted.astype(jnp.bfloat16), 'ep', scatter_dimension=1...  18.8 us
    dot_general x1, matrix products, shards(): gate_act = jnp.dot(row_block, gate_w, preferred_element_type=jnp.float32)  7.86 us
    unnamed x12, local copies, waits for them, and re-layouts  6.35 us
  transfers between devices with their start and end apart: 3, of which 3 were waited for; matrix products, arithmetic and copies ran while one was open for 1% of the time, Pallas kernels for 0%

commit v1 on v0

v1 whole, which is shorter than its diff:
```python
import functools

import jax
import jax.numpy as jnp
from jax import lax
from jax.experimental import pallas as pl
from jax.experimental.pallas import tpu as pltpu
from jax.sharding import PartitionSpec as P

SLOT = 36
MAIN = 32
REST = SLOT - MAIN
PACK = MAIN // REST
PAIR = 2 * MAIN + 16
F32 = jnp.float32
BF16 = jnp.bfloat16


def mm(a, b, dims=((1,), (0,))):
    return lax.dot_general(a, b, (dims, ((), ())), preferred_element_type=F32)


def one_hot(rows, cols, test):
    r = lax.broadcasted_iota(jnp.int32, (rows, cols), 0)
    c = lax.broadcasted_iota(jnp.int32, (rows, cols), 1)
    return jnp.where(test(r, c), 1.0, 0.0).astype(BF16)


def kernel(
    n, tok, ids, wts, bits, wg_hbm, wu_hbm, wd_hbm, out,
    wg, wu, wd, X, xl, h, pb, yr, zr, em, ex,
    wsem, sR, sL, sY, rz, ry, sYr, rYr, sZ, rL, rR, se, re,
):
    nz = n // 2
    t = lax.axis_index("tp")
    e = lax.axis_index("ep")
    z, y = t // 2, t % 2
    D = tok.shape[1]
    CH = D // PACK
    F = wg.shape[1]
    TOK = tok.shape[0]
    partner = t + 1 - 2 * y
    first, last = z == 0, z == nz - 1

    loads = [
        pltpu.make_async_copy(a.at[0], b, wsem.at[i])
        for i, (a, b) in enumerate(((wg_hbm, wg), (wu_hbm, wu), (wd_hbm, wd)))
    ]
    for c in loads:
        c.start()

    barrier = pltpu.get_barrier_semaphore()
    pl.semaphore_signal(barrier, inc=1, device_id={"tp": partner})
    pl.semaphore_signal(barrier, inc=1, device_id={"ep": 1 - e})

    @pl.when(jnp.logical_not(first))
    def _():
        pl.semaphore_signal(barrier, inc=1, device_id={"tp": t - 2})

    @pl.when(jnp.logical_not(last))
    def _():
        pl.semaphore_signal(barrier, inc=1, device_id={"tp": t + 2})

    tri = one_hot(TOK, TOK, lambda r, c: c <= r)

    def routing(expert):
        hit = ids[...] == expert
        share = jnp.sum(jnp.where(hit, wts[...], 0.0), axis=1, keepdims=True)
        named = jnp.sum(jnp.where(hit, 1.0, 0.0), axis=1, keepdims=True)
        named = jnp.broadcast_to(named, (TOK, TOK))
        count = mm(tri, named.astype(BF16))
        row = jnp.where(named > 0.5, count, 0.0).astype(jnp.int32) - 1
        return share, row

    def main_hot(row):
        c = lax.broadcasted_iota(jnp.int32, (TOK, MAIN), 1)
        return jnp.where(row[:, :MAIN] == c, 1.0, 0.0).astype(BF16)

    def rest_hot(row, q, width):
        c = lax.broadcasted_iota(jnp.int32, (TOK, width), 1)
        here = (c >= REST * q) & (c < REST * q + REST)
        return jnp.where(here & (row[:, :width] - MAIN == c - REST * q), 1.0, 0.0).astype(BF16)

    _, row = routing(e)
    hot = main_hot(row)
    rest = jnp.zeros((MAIN, CH), F32)
    for q in range(PACK):
        part = tok[:, q * CH:(q + 1) * CH]
        X[t, :, q * CH:(q + 1) * CH] = mm(hot, part, ((0,), (0,))).astype(BF16)
        rest = rest + mm(rest_hot(row, q, MAIN), part, ((0,), (0,)))
    X[t, :, D:] = rest.astype(BF16)

    neighbours = 4 - first.astype(jnp.int32) - last.astype(jnp.int32)
    pl.semaphore_wait(barrier, neighbours)

    def go_right(b):
        i = 2 * b + y
        return pltpu.make_async_remote_copy(X.at[i], X.at[i], sR.at[b], rz.at[b], device_id={"tp": t + 2})

    def go_left(b):
        i = 2 * b + y
        return pltpu.make_async_remote_copy(X.at[i], X.at[i], sL.at[b], rz.at[b], device_id={"tp": t - 2})

    def go_y(b):
        i = 2 * b + y
        return pltpu.make_async_remote_copy(X.at[i], X.at[i], sY.at[b], ry.at[b], device_id={"tp": partner})

    @pl.when(jnp.logical_not(last))
    def _():
        go_right(z).start()

    @pl.when(jnp.logical_not(first))
    def _():
        go_left(z).start()

    go_y(z).start()

    def arrivals(d):
        a, b = z - d, z + d

        @pl.when(a >= 0)
        def _():
            go_right(a).wait_recv()

            @pl.when(jnp.logical_not(last))
            def _():
                go_right(a).start()

            go_y(a).start()

        @pl.when(b < nz)
        def _():
            go_left(b).wait_recv()

            @pl.when(jnp.logical_not(first))
            def _():
                go_left(b).start()

            go_y(b).start()

    def place(j):
        d = (j + 1) // 2
        return jnp.where(j % 2 == 1, z - d, z + d)

    def hidden(b):
        go_y(b).wait_recv()
        packed = X[pl.ds(2 * b, 2), :, D:].reshape(2 * MAIN, CH)
        for q in range(PACK):
            pick = one_hot(16, 2 * MAIN, lambda r, c: (r < 2 * REST) & (c == (r // REST) * MAIN + REST * q + r % REST))
            cols = slice(q * CH, (q + 1) * CH)
            xl[:2 * MAIN, cols] = X[pl.ds(2 * b, 2), :, cols].reshape(2 * MAIN, CH)
            xl[2 * MAIN:, cols] = mm(pick, packed).astype(BF16)

        def tile(i, _):
            cols = pl.ds(pl.multiple_of(i * 256, 256), 256)
            g = mm(xl[...], wg[:, cols])
            u = mm(xl[...], wu[:, cols])
            h[b, :, cols] = ((g / (1.0 + jnp.exp(-g))) * u).astype(BF16)
            return 0

        lax.fori_loop(0, F // 256, tile, 0)

    arrivals(1)
    loads[0].wait()
    loads[1].wait()

    def gather_step(j, _):
        d = (j + 1) // 2 + 1

        @pl.when((j % 2 == 1) & (d < nz))
        def _():
            arrivals(d)

        b = place(j)

        @pl.when((b >= 0) & (b < nz))
        def _():
            hidden(b)

        return 0

    lax.fori_loop(0, 2 * nz - 1, gather_step, 0)
    loads[2].wait()

    def give_y(b):
        return pltpu.make_async_remote_copy(
            pb.at[2 * b + 1 - y], yr.at[b], sYr.at[b], rYr.at[b], device_id={"tp": partner})

    def give_right(b):
        return pltpu.make_async_remote_copy(
            pb.at[2 * b + y], zr.at[b + 1], sZ.at[b], rL.at[b], device_id={"tp": t + 2})

    def give_left(b):
        return pltpu.make_async_remote_copy(
            pb.at[2 * b + y], zr.at[b], sZ.at[b], rR.at[b], device_id={"tp": t - 2})

    def down(b):
        rest = jnp.zeros((2 * MAIN, CH), F32)
        for q in range(PACK):
            cols = slice(q * CH, (q + 1) * CH)
            part = mm(h[b], wd[:, cols])
            c = lax.broadcasted_iota(jnp.int32, (PAIR, CH), 1) + q * CH
            low = (bits[b] + 40503 * c) & 65535
            part = (part * (0.5 + low.astype(F32) / 65536.0)).astype(BF16)
            pb[pl.ds(2 * b, 2), :, cols] = part[:2 * MAIN].reshape(2, MAIN, CH)
            put = one_hot(2 * MAIN, 16, lambda r, c: (c < 2 * REST) & (r == (c // REST) * MAIN + REST * q + c % REST))
            rest = rest + mm(put, part[2 * MAIN:])
        pb[pl.ds(2 * b, 2), :, D:] = rest.astype(BF16).reshape(2, MAIN, CH)
        give_y(b).start()

    def down_step(i, _):
        b = place(2 * nz - 2 - i)

        @pl.when((b >= 0) & (b < nz))
        def _():
            down(b)

        return 0

    lax.fori_loop(0, 2 * nz - 1, down_step, 0)

    def add_all(i, more):
        for q in range(PACK + 1):
            cols = slice(q * CH, (q + 1) * CH)
            total = pb[i, :, cols].astype(F32)
            for ref, k in more:
                total = total + ref[k, :, cols].astype(F32)
            pb[i, :, cols] = total.astype(BF16)

    def reduce_step(i, _):
        b = place(2 * nz - 2 - i)
        mine = 2 * b + y

        @pl.when((b >= 0) & (b < nz))
        def _():
            give_y(b).wait_recv()

            @pl.when((b >= z) & jnp.logical_not(first))
            def _():
                give_right(b).wait_recv()

            @pl.when((b <= z) & jnp.logical_not(last))
            def _():
                give_left(b).wait_recv()

            @pl.when(((b > z) & first) | ((b < z) & last))
            def _():
                add_all(mine, ((yr, b),))

            @pl.when(((b > z) & jnp.logical_not(first)) | ((b == z) & last))
            def _():
                add_all(mine, ((yr, b), (zr, b + 1)))

            @pl.when(((b < z) & jnp.logical_not(last)) | ((b == z) & first))
            def _():
                add_all(mine, ((yr, b), (zr, b)))

            @pl.when((b == z) & jnp.logical_not(first) & jnp.logical_not(last))
            def _():
                add_all(mine, ((yr, b), (zr, b + 1), (zr, b)))

            @pl.when(b > z)
            def _():
                give_right(b).start()

            @pl.when(b < z)
            def _():
                give_left(b).start()

        return 0

    lax.fori_loop(0, 2 * nz - 1, reduce_step, 0)

    half = D // 2
    theirs = pl.ds(pl.multiple_of((1 - e) * half, 128), half)
    give_main = pltpu.make_async_remote_copy(
        pb.at[t, :, theirs], em, se.at[0], re.at[0], device_id={"ep": 1 - e})
    give_rest = pltpu.make_async_remote_copy(
        pb.at[t, pl.ds(pl.multiple_of((1 - e) * 16, 16), 16), D:], ex, se.at[1], re.at[1], device_id={"ep": 1 - e})
    give_main.start()
    give_rest.start()
    share0, row0 = routing(e)
    share1, row1 = routing(1 - e)
    hot0, hot1 = main_hot(row0), main_hot(row1)
    give_main.wait_recv()
    give_rest.wait_recv()
    rest0 = pb[t, pl.ds(pl.multiple_of(e * 16, 16), 16), D:]
    rest1 = ex[...]
    for q in range(PACK // 2):
        cols = slice(q * CH, (q + 1) * CH)
        own = pl.ds(pl.multiple_of(e * half + q * CH, 128), CH)
        a = mm(hot0, pb[t, :, own]) + mm(rest_hot(row0, q, 16), rest0)
        b = mm(hot1, em[:, cols]) + mm(rest_hot(row1, q, 16), rest1)
        out[:, cols] = (share0 * a + share1 * b).astype(BF16)

    give_main.wait_send()
    give_rest.wait_send()

    def finish(b, _):
        go_y(b).wait_send()
        give_y(b).wait_send()

        @pl.when((b <= z) & jnp.logical_not(last))
        def _():
            go_right(b).wait_send()

        @pl.when((b >= z) & jnp.logical_not(first))
        def _():
            go_left(b).wait_send()

        @pl.when(b > z)
        def _():
            give_right(b).wait_send()

        @pl.when(b < z)
        def _():
            give_left(b).wait_send()

        return 0

    lax.fori_loop(0, nz, finish, 0)


def shards(n, tokens, expert_ids, route_weight, w_gate, w_up, w_down, round_bits):
    nz = n // 2
    D = tokens.shape[1]
    F = w_gate.shape[2]
    wide = D + D // PACK
    rows = round_bits.reshape(nz, 2, SLOT)
    main = rows[:, :, :MAIN].reshape(nz, 2 * MAIN)
    rest = rows[:, :, MAIN:].reshape(nz, 2 * REST)
    bits = jnp.concatenate([main, rest, jnp.zeros((nz, 16 - 2 * REST), jnp.int32)], axis=1)[:, :, None]
    vmem = pl.BlockSpec(memory_space=pltpu.VMEM)
    hbm = pl.BlockSpec(memory_space=pl.ANY)
    dma = pltpu.SemaphoreType.DMA
    return pl.pallas_call(
        functools.partial(kernel, n),
        out_shape=jax.ShapeDtypeStruct((tokens.shape[0], D // 2), BF16),
        in_specs=[vmem] * 4 + [hbm] * 3,
        out_specs=vmem,
        scratch_shapes=[
            pltpu.VMEM((D, F), BF16),
            pltpu.VMEM((D, F), BF16),
            pltpu.VMEM((F, D), BF16),
            pltpu.VMEM((n, MAIN, wide), BF16),
            pltpu.VMEM((PAIR, D), BF16),
            pltpu.VMEM((nz, PAIR, F), BF16),
            pltpu.VMEM((n, MAIN, wide), BF16),
            pltpu.VMEM((nz, MAIN, wide), BF16),
            pltpu.VMEM((nz + 1, MAIN, wide), BF16),
            pltpu.VMEM((MAIN, D // 2), BF16),
            pltpu.VMEM((16, D // PACK), BF16),
            dma((3,)),
        ] + [dma((nz,))] * 10 + [dma((2,))] * 2,
        compiler_params=pltpu.CompilerParams(
            collective_id=0, has_side_effects=True, vmem_limit_bytes=62 * 2**20
        ),
        cost_estimate=pl.CostEstimate(
            flops=6 * n * SLOT * D * F, bytes_accessed=6 * D * F, transcendentals=n * SLOT * F
        ),
    )(tokens, expert_ids, route_weight, bits, w_gate, w_up, w_down)


def solution(mesh):
    return jax.shard_map(
        functools.partial(shards, mesh.shape["tp"]),
        mesh=mesh,
        in_specs=(
            P(("parts", "tp"), None),
            P(("parts", "tp"), None),
            P(("parts", "tp"), None),
            P("ep", None, "tp"),
            P("ep", None, "tp"),
            P("ep", "tp", None),
            P("ep", "tp", None),
        ),
        out_specs=P(("parts", "tp"), "ep"),
        check_vma=False,
    )
```

time: 230 us -> 106 us (0.46)
  Pallas kernels: 0 us -> 98.6 us
  waiting for transfers between devices: 93.1 us -> 0 us
  blocking collectives: 77.6 us -> 0 us
  matrix products: 31.9 us -> 0 us
  between operations: 14.1 us -> 0.01 us
  starting transfers between devices: 4.17 us -> 0 us
    pallas_call x0 -> x1, Pallas kernels: none -> 98.6 us  [shards(): pl.pallas_call(functools.partial(kernel, n), out_shape=jax.ShapeDtypeStru...]
    unnamed x1 -> x0, blocking collectives: 77.6 us -> none
    all_gather x1 -> x0, waiting for transfers between devices: 70.8 us -> none  [shards(): row_block = lax.all_gather(outgoing, 'tp', axis=0, tiled=True)]
    dot_general x4 -> x0, matrix products: 31.9 us -> none  [the longest x1 21.1 us: shards(): partial_value = jnp.dot(hidden, down_w, preferred_element_type=jnp.float32)]
    reduce_scatter x1 -> x0, waiting for transfers between devices: 18.8 us -> none  [shards(): lax.psum_scatter(weighted.astype(jnp.bfloat16), 'ep', scatter_dimension=1...]
    unnamed x1 -> x0, starting transfers between devices: 4.13 us -> none
    unnamed x3 -> x0, waiting for transfers between devices: 3.42 us -> none
    unnamed x12 -> x3, local copies, waits for them, and re-layouts: 6.35 us -> 4.87 us
  transfers between devices with their start and end apart: 3 -> 0, of which waited for: 3 -> 0; matrix products, arithmetic and copies ran while one was open for 1% -> 0% of each run, Pallas kernels for 0% -> 0%
where the time goes in v1:
time: 106 us; the launch traced here: 105 us
  Pallas kernels  98.6 us (93%)
  local copies, waits for them, and re-layouts  6.07 us (6%)
    pallas_call x1, Pallas kernels, shards(): pl.pallas_call(functools.partial(kernel, n), out_shape=jax.ShapeDtypeStru...  98.6 us
    unnamed x3, local copies, waits for them, and re-layouts  4.87 us

profile of v1, /device:TPU:1, one launch (start us, length us, event | category | flops | bytes accessed | tf_op | source)
XLA Modules:
  0.0 105.5 jit_solution(9528122730418668333)
XLA Ops:
  0.0 0.1 pad.2.clone
  0.1 0.7 reduce
  0.8 0.1 reshape.9
  0.9 0.1 reshape.10
  1.0 0.1 slice.9
  1.0 0.1 reshape.11
  1.1 0.1 add_bitcast_fusion
  1.2 1.4 %copy.10.ids = s32[128,2]{1,0:T(8,128)} copy(s32[128,2]{0,1:T(2,128)} %param.8) | data formatting | bytes 2048 | tf_op args[1]
  2.6 1.4 %copy.11.wts = f32[128,2]{1,0:T(8,128)} copy(f32[128,2]{0,1:T(2,128)} %param.9) | data formatting | bytes 2048 | tf_op args[2]
  4.0 0.8 copy.12.bits
  4.8 98.6 %shard_map.73 = bf16[128,3072]{1,0:T(8,128)(2,1)} custom-call(bf16[128,6144]{1,0:T(8,128)(2,1)} %tok.1, s32[128,2]{1,0:T(8,128)} %copy.10.ids, f32[128,2]{1,0:T(8,128)} %copy.11.wts, s32[4,80,1]{2,1,0:T(8,128)} %copy.12.bits, bf16[1,6144,1024]{2,1,0:T(8,128)(2,1)} %wg_hbm.1, bf16[1,6144,1024]{2,1,0:T(8,128)(2,1)} %wu_hbm.1, bf16[1,1024,6144]{2,1,0:T(8,128)(2,1)} %wd_hbm.1), custom_call_target="tpu_custom_call" | custom-call | flops 10871635968 | bytes 37748736 | tf_op jit(solution)/shard_map/pallas_call | solution.py:336
  103.4 2.1 %copy.14 = bf16[128,3072]{1,0:T(8,128)(2,1)} copy(bf16[128,3072]{1,0:T(8,128)(2,1)} %shard_map.73) | data formatting | bytes 1572864
  (1 shorter events, 0.0 us)

commit v2 on v1

--- a/solution.py
+++ b/solution.py
@@ -27,9 +27,9 @@
 
 
 def kernel(
-    n, tok, ids, wts, bits, wg_hbm, wu_hbm, wd_hbm, out,
-    wg, wu, wd, X, xl, h, pb, yr, zr, em, ex,
-    wsem, sR, sL, sY, rz, ry, sYr, rYr, sZ, rL, rR, se, re,
+    n, cut, tok, ids, wts, bits, wg_hbm, wu_hbm, wd_hbm, out,
+    wg, wu, wd, X, xl, h, pb, yr, zr, zt, yt, em, ex,
+    wsem, sR, sL, sY, rz, ry, sYr, rYr, sZ, rL, rR, sRt, sLt, rzt, sZt, rLt, rRt, st, rt, se, re,
 ):
     nz = n // 2
     t = lax.axis_index("tp")
@@ -65,9 +65,10 @@
 
     def routing(expert):
         hit = ids[...] == expert
-        share = jnp.sum(jnp.where(hit, wts[...], 0.0), axis=1, keepdims=True)
-        named = jnp.sum(jnp.where(hit, 1.0, 0.0), axis=1, keepdims=True)
-        named = jnp.broadcast_to(named, (TOK, TOK))
+        share = jnp.sum(jnp.where(hit, wts[...], 0.0), axis=0, keepdims=True)
+        named = jnp.sum(jnp.where(hit, 1.0, 0.0), axis=0, keepdims=True)
+        share = jnp.broadcast_to(share, (TOK, TOK)).T[:, :1]
+        named = jnp.broadcast_to(named, (TOK, TOK)).T
         count = mm(tri, named.astype(BF16))
         row = jnp.where(named > 0.5, count, 0.0).astype(jnp.int32) - 1
         return share, row
@@ -103,7 +104,25 @@
 
     def go_y(b):
         i = 2 * b + y
-        return pltpu.make_async_remote_copy(X.at[i], X.at[i], sY.at[b], ry.at[b], device_id={"tp": partner})
+        return pltpu.make_async_remote_copy(
+            X.at[i, :, :cut], X.at[i, :, :cut], sY.at[b], ry.at[b], device_id={"tp": partner})
+
+    def tail_y():
+        return pltpu.make_async_remote_copy(
+            X.at[t, :, cut:], X.at[t, :, cut:], st.at[0], rt.at[0], device_id={"tp": partner})
+
+    def tail_right(b):
+        i = 2 * b + 1 - y
+        return pltpu.make_async_remote_copy(
+            X.at[i, :, cut:], X.at[i, :, cut:], sRt.at[b], rzt.at[b], device_id={"tp": t + 2})
+
+    def tail_left(b):
+        i = 2 * b + 1 - y
+        return pltpu.make_async_remote_copy(
+            X.at[i, :, cut:], X.at[i, :, cut:], sLt.at[b], rzt.at[b], device_id={"tp": t - 2})
+
+    tail_y().start()
+    go_y(z).start()
 
     @pl.when(jnp.logical_not(last))
     def _():
@@ -113,7 +132,15 @@
     def _():
         go_left(z).start()
 
-    go_y(z).start()
+    tail_y().wait_recv()
+
+    @pl.when(jnp.logical_not(last))
+    def _():
+        tail_right(z).start()
+
+    @pl.when(jnp.logical_not(first))
+    def _():
+        tail_left(z).start()
 
     def arrivals(d):
         a, b = z - d, z + d
@@ -127,6 +154,11 @@
                 go_right(a).start()
 
             go_y(a).start()
+            tail_right(a).wait_recv()
+
+            @pl.when(jnp.logical_not(last))
+            def _():
+                tail_right(a).start()
 
         @pl.when(b < nz)
         def _():
@@ -137,6 +169,11 @@
                 go_left(b).start()
 
             go_y(b).start()
+            tail_left(b).wait_recv()
+
+            @pl.when(jnp.logical_not(first))
+            def _():
+                tail_left(b).start()
 
     def place(j):
         d = (j + 1) // 2
@@ -184,7 +221,7 @@
 
     def give_y(b):
         return pltpu.make_async_remote_copy(
-            pb.at[2 * b + 1 - y], yr.at[b], sYr.at[b], rYr.at[b], device_id={"tp": partner})
+            pb.at[2 * b + 1 - y, :, :cut], yr.at[b], sYr.at[b], rYr.at[b], device_id={"tp": partner})
 
     def give_right(b):
         return pltpu.make_async_remote_copy(
@@ -194,13 +231,39 @@
         return pltpu.make_async_remote_copy(
             pb.at[2 * b + y], zr.at[b], sZ.at[b], rR.at[b], device_id={"tp": t - 2})
 
+    def tail_give_right(b):
+        return pltpu.make_async_remote_copy(
+            pb.at[2 * b + 1 - y, :, cut:], zt.at[b + 1], sZt.at[b], rLt.at[b], device_id={"tp": t + 2})
+
+    def tail_give_left(b):
+        return pltpu.make_async_remote_copy(
+            pb.at[2 * b + 1 - y, :, cut:], zt.at[b], sZt.at[b], rRt.at[b], device_id={"tp": t - 2})
+
+    def tail_give_y():
+        return pltpu.make_async_remote_copy(
+            pb.at[partner, :, cut:], yt, st.at[1], rt.at[1], device_id={"tp": partner})
+
+    low16 = (bits[0] & 65535).astype(F32)
+
+    def row_noise(b):
+        shape = (PAIR, n * SLOT)
+        r = lax.broadcasted_iota(jnp.int32, shape, 0)
+        c = lax.broadcasted_iota(jnp.int32, shape, 1) - 2 * SLOT * b
+        k = r - 2 * MAIN
+        main = (r // MAIN) * SLOT + r % MAIN
+        rest = (k // REST) * SLOT + MAIN + k % REST
+        source = jnp.where(r < 2 * MAIN, main, jnp.where(k < 2 * REST, rest, -n * SLOT - 1))
+        picked = jnp.where(source == c, jnp.broadcast_to(low16, shape), 0.0)
+        return jnp.sum(picked, axis=1, keepdims=True).astype(jnp.int32)
+
     def down(b):
+        noise = row_noise(b)
         rest = jnp.zeros((2 * MAIN, CH), F32)
         for q in range(PACK):
             cols = slice(q * CH, (q + 1) * CH)
             part = mm(h[b], wd[:, cols])
             c = lax.broadcasted_iota(jnp.int32, (PAIR, CH), 1) + q * CH
-            low = (bits[b] + 40503 * c) & 65535
+            low = (noise + 40503 * c) & 65535
             part = (part * (0.5 + low.astype(F32) / 65536.0)).astype(BF16)
             pb[pl.ds(2 * b, 2), :, cols] = part[:2 * MAIN].reshape(2, MAIN, CH)
             put = one_hot(2 * MAIN, 16, lambda r, c: (c < 2 * REST) & (r == (c // REST) * MAIN + REST * q + c % REST))
@@ -208,68 +271,118 @@
         pb[pl.ds(2 * b, 2), :, D:] = rest.astype(BF16).reshape(2, MAIN, CH)
         give_y(b).start()
 
+    def add_in(i, start, stop, terms):
+        for c in range(start, stop, 384):
+            size = min(384, stop - c)
+            total = pb[i, :, c:c + size].astype(F32)
+            for ref, k, base in terms:
+                total = total + ref[k, :, c - base:c - base + size].astype(F32)
+            pb[i, :, c:c + size] = total.astype(BF16)
+
+    wide = pb.shape[2]
+
+    def reduce(b):
+        mine, other = 2 * b + y, 2 * b + 1 - y
+        from_left = (b >= z) & jnp.logical_not(first)
+        from_right = (b <= z) & jnp.logical_not(last)
+        only_left = from_left & jnp.logical_not(from_right)
+        only_right = from_right & jnp.logical_not(from_left)
+        both = from_left & from_right
+        none = jnp.logical_not(from_left) & jnp.logical_not(from_right)
+
+        @pl.when(from_left)
+        def _():
+            tail_give_right(b).wait_recv()
+
+        @pl.when(from_right)
+        def _():
+            tail_give_left(b).wait_recv()
+
+        @pl.when(only_left)
+        def _():
+            add_in(other, cut, wide, ((zt, b + 1, cut),))
+
+        @pl.when(only_right)
+        def _():
+            add_in(other, cut, wide, ((zt, b, cut),))
+
+        @pl.when(both)
+        def _():
+            add_in(other, cut, wide, ((zt, b + 1, cut), (zt, b, cut)))
+
+        @pl.when(b > z)
+        def _():
+            tail_give_right(b).start()
+
+        @pl.when(b < z)
+        def _():
+            tail_give_left(b).start()
+
+        @pl.when(b == z)
+        def _():
+            tail_give_y().start()
+
+        give_y(b).wait_recv()
+
+        @pl.when(from_left)
+        def _():
+            give_right(b).wait_recv()
+
+        @pl.when(from_right)
+        def _():
+            give_left(b).wait_recv()
+
+        @pl.when(none)
+        def _():
+            add_in(mine, 0, cut, ((yr, b, 0),))
+
+        @pl.when(only_left)
+        def _():
+            add_in(mine, 0, cut, ((yr, b, 0), (zr, b + 1, 0)))
+            add_in(mine, cut, wide, ((zr, b + 1, 0),))
+
+        @pl.when(only_right)
+        def _():
+            add_in(mine, 0, cut, ((yr, b, 0), (zr, b, 0)))
+            add_in(mine, cut, wide, ((zr, b, 0),))
+
+        @pl.when(both)
+        def _():
+            add_in(mine, 0, cut, ((yr, b, 0), (zr, b + 1, 0), (zr, b, 0)))
+            add_in(mine, cut, wide, ((zr, b + 1, 0), (zr, b, 0)))
+
+        @pl.when(b > z)
+        def _():
+            give_right(b).start()
+
+        @pl.when(b < z)
+        def _():
+            give_left(b).start()
+
+    steps, lag = 2 * nz - 1, 3
+
     def down_step(i, _):
-        b = place(2 * nz - 2 - i)
-
-        @pl.when((b >= 0) & (b < nz))
+        b = place(jnp.maximum(steps - 1 - i, 0))
+
+        @pl.when((i < steps) & (b >= 0) & (b < nz))
         def _():
             down(b)
 
+        k = place(jnp.minimum(steps - 1 - i + lag, steps - 1))
+
+        @pl.when((i >= lag) & (k >= 0) & (k < nz))
+        def _():
+            reduce(k)
+
         return 0
 
-    lax.fori_loop(0, 2 * nz - 1, down_step, 0)
-
-    def add_all(i, more):
-        for q in range(PACK + 1):
-            cols = slice(q * CH, (q + 1) * CH)
-            total = pb[i, :, cols].astype(F32)
-            for ref, k in more:
-                total = total + ref[k, :, cols].astype(F32)
-            pb[i, :, cols] = total.astype(BF16)
-
-    def reduce_step(i, _):
-        b = place(2 * nz - 2 - i)
-        mine = 2 * b + y
-
-        @pl.when((b >= 0) & (b < nz))
-        def _():
-            give_y(b).wait_recv()
-
-            @pl.when((b >= z) & jnp.logical_not(first))
-            def _():
-                give_right(b).wait_recv()
-
-            @pl.when((b <= z) & jnp.logical_not(last))
-            def _():
-                give_left(b).wait_recv()
-
-            @pl.when(((b > z) & first) | ((b < z) & last))
-            def _():
-                add_all(mine, ((yr, b),))
-
-            @pl.when(((b > z) & jnp.logical_not(first)) | ((b == z) & last))
-            def _():
-                add_all(mine, ((yr, b), (zr, b + 1)))
-
-            @pl.when(((b < z) & jnp.logical_not(last)) | ((b == z) & first))
-            def _():
-                add_all(mine, ((yr, b), (zr, b)))
-
-            @pl.when((b == z) & jnp.logical_not(first) & jnp.logical_not(last))
-            def _():
-                add_all(mine, ((yr, b), (zr, b + 1), (zr, b)))
-
-            @pl.when(b > z)
-            def _():
-                give_right(b).start()
-
-            @pl.when(b < z)
-            def _():
-                give_left(b).start()
-
-        return 0
-
-    lax.fori_loop(0, 2 * nz - 1, reduce_step, 0)
+    lax.fori_loop(0, steps + lag, down_step, 0)
+    tail_give_y().wait_recv()
+    for c in range(cut, wide, 384):
+        size = min(384, wide - c)
+        pb[t, :, c:c + size] = (
+            pb[t, :, c:c + size].astype(F32) + yt[:, c - cut:c - cut + size].astype(F32)
+        ).astype(BF16)
 
     half = D // 2
     theirs = pl.ds(pl.multiple_of((1 - e) * half, 128), half)
@@ -296,6 +409,9 @@
     give_main.wait_send()
     give_rest.wait_send()
 
+    tail_y().wait_send()
+    tail_give_y().wait_send()
+
     def finish(b, _):
         go_y(b).wait_send()
         give_y(b).wait_send()
@@ -303,18 +419,22 @@
         @pl.when((b <= z) & jnp.logical_not(last))
         def _():
             go_right(b).wait_send()
+            tail_right(b).wait_send()
 
         @pl.when((b >= z) & jnp.logical_not(first))
         def _():
             go_left(b).wait_send()
+            tail_left(b).wait_send()
 
         @pl.when(b > z)
         def _():
             give_right(b).wait_send()
+            tail_give_right(b).wait_send()
 
         @pl.when(b < z)
         def _():
             give_left(b).wait_send()
+            tail_give_left(b).wait_send()
 
         return 0
 
@@ -326,15 +446,12 @@
     D = tokens.shape[1]
     F = w_gate.shape[2]
     wide = D + D // PACK
-    rows = round_bits.reshape(nz, 2, SLOT)
-    main = rows[:, :, :MAIN].reshape(nz, 2 * MAIN)
-    rest = rows[:, :, MAIN:].reshape(nz, 2 * REST)
-    bits = jnp.concatenate([main, rest, jnp.zeros((nz, 16 - 2 * REST), jnp.int32)], axis=1)[:, :, None]
+    cut = wide - wide // 128 // 6 * 128
     vmem = pl.BlockSpec(memory_space=pltpu.VMEM)
     hbm = pl.BlockSpec(memory_space=pl.ANY)
     dma = pltpu.SemaphoreType.DMA
     return pl.pallas_call(
-        functools.partial(kernel, n),
+        functools.partial(kernel, n, cut),
         out_shape=jax.ShapeDtypeStruct((tokens.shape[0], D // 2), BF16),
         in_specs=[vmem] * 4 + [hbm] * 3,
         out_specs=vmem,
@@ -346,19 +463,21 @@
             pltpu.VMEM((PAIR, D), BF16),
             pltpu.VMEM((nz, PAIR, F), BF16),
             pltpu.VMEM((n, MAIN, wide), BF16),
-            pltpu.VMEM((nz, MAIN, wide), BF16),
+            pltpu.VMEM((nz, MAIN, cut), BF16),
             pltpu.VMEM((nz + 1, MAIN, wide), BF16),
+            pltpu.VMEM((nz + 1, MAIN, wide - cut), BF16),
+            pltpu.VMEM((MAIN, wide - cut), BF16),
             pltpu.VMEM((MAIN, D // 2), BF16),
             pltpu.VMEM((16, D // PACK), BF16),
             dma((3,)),
-        ] + [dma((nz,))] * 10 + [dma((2,))] * 2,
+        ] + [dma((nz,))] * 16 + [dma((2,))] * 4,
         compiler_params=pltpu.CompilerParams(
             collective_id=0, has_side_effects=True, vmem_limit_bytes=62 * 2**20
         ),
         cost_estimate=pl.CostEstimate(
             flops=6 * n * SLOT * D * F, bytes_accessed=6 * D * F, transcendentals=n * SLOT * F
         ),
-    )(tokens, expert_ids, route_weight, bits, w_gate, w_up, w_down)
+    )(tokens, expert_ids.T, route_weight.T, round_bits, w_gate, w_up, w_down)
 
 
 def solution(mesh):

time: 106 us -> 103 us (0.972)
  local copies, waits for them, and re-layouts: 6.07 us -> 2.06 us
  Pallas kernels: 98.6 us -> 101 us
    unnamed x3 -> x1, local copies, waits for them, and re-layouts: 4.87 us -> 2.06 us
    pallas_call x1, Pallas kernels: 98.6 us -> 101 us  [shards(): pl.pallas_call(functools.partial(kernel, n, cut), out_shape=jax.ShapeDtyp...]
where the time goes in v2:
time: 103 us
  Pallas kernels  101 us (98%)
  local copies, waits for them, and re-layouts  2.06 us (2%)
    pallas_call x1, Pallas kernels, shards(): pl.pallas_call(functools.partial(kernel, n, cut), out_shape=jax.ShapeDtyp...  101 us
    unnamed x1, local copies, waits for them, and re-layouts  2.06 us

profile of v2, /device:TPU:1, one launch (start us, length us, event | category | flops | bytes accessed | tf_op | source)
XLA Modules:
  0.0 102.7 jit_solution(714311089159445096)
XLA Ops:
  0.0 100.7 %shard_map.73 = bf16[128,3072]{1,0:T(8,128)(2,1)} custom-call(bf16[128,6144]{1,0:T(8,128)(2,1)} %tok.1, s32[2,128]{1,0:T(2,128)} %bitcast.2, f32[2,128]{1,0:T(2,128)} %bitcast.3, s32[1,1,288]{2,1,0:T(1,128)} %bits.1, bf16[1,6144,1024]{2,1,0:T(8,128)(2,1)} %wg_hbm.1, bf16[1,6144,1024]{2,1,0:T(8,128)(2,1)} %wu_hbm.1, bf16[1,1024,6144]{2,1,0:T(8,128)(2,1)} %wd_hbm.1), custom_call_target="tpu_custom_call" | custom-call | flops 10871635968 | bytes 37748736 | tf_op jit(solution)/shard_map/pallas_call | solution.py:453
  100.7 2.1 %copy.9 = bf16[128,3072]{1,0:T(8,128)(2,1)} copy(bf16[128,3072]{1,0:T(8,128)(2,1)} %shard_map.73) | data formatting | bytes 1572864

commit v3 on v2

--- a/solution.py
+++ b/solution.py
@@ -11,6 +11,7 @@
 MAIN = 32
 REST = SLOT - MAIN
 PACK = MAIN // REST
+CHUNKS = 3
 PAIR = 2 * MAIN + 16
 F32 = jnp.float32
 BF16 = jnp.bfloat16
@@ -94,18 +95,22 @@
     neighbours = 4 - first.astype(jnp.int32) - last.astype(jnp.int32)
     pl.semaphore_wait(barrier, neighbours)
 
-    def go_right(b):
-        i = 2 * b + y
-        return pltpu.make_async_remote_copy(X.at[i], X.at[i], sR.at[b], rz.at[b], device_id={"tp": t + 2})
-
-    def go_left(b):
-        i = 2 * b + y
-        return pltpu.make_async_remote_copy(X.at[i], X.at[i], sL.at[b], rz.at[b], device_id={"tp": t - 2})
-
-    def go_y(b):
-        i = 2 * b + y
-        return pltpu.make_async_remote_copy(
-            X.at[i, :, :cut], X.at[i, :, :cut], sY.at[b], ry.at[b], device_id={"tp": partner})
+    step = cut // CHUNKS
+
+    def span(k):
+        return slice(k * step, (k + 1) * step) if k < CHUNKS else slice(cut, X.shape[2])
+
+    def go_right(b, k):
+        ref = X.at[2 * b + y, :, span(k)]
+        return pltpu.make_async_remote_copy(ref, ref, sR.at[b, k], rz.at[b, k], device_id={"tp": t + 2})
+
+    def go_left(b, k):
+        ref = X.at[2 * b + y, :, span(k)]
+        return pltpu.make_async_remote_copy(ref, ref, sL.at[b, k], rz.at[b, k], device_id={"tp": t - 2})
+
+    def go_y(b, k):
+        ref = X.at[2 * b + y, :, span(k)]
+        return pltpu.make_async_remote_copy(ref, ref, sY.at[b, k], ry.at[b, k], device_id={"tp": partner})
 
     def tail_y():
         return pltpu.make_async_remote_copy(
@@ -122,15 +127,17 @@
             X.at[i, :, cut:], X.at[i, :, cut:], sLt.at[b], rzt.at[b], device_id={"tp": t - 2})
 
     tail_y().start()
-    go_y(z).start()
-
-    @pl.when(jnp.logical_not(last))
-    def _():
-        go_right(z).start()
-
-    @pl.when(jnp.logical_not(first))
-    def _():
-        go_left(z).start()
+    for k in range(CHUNKS + 1):
+        @pl.when(jnp.logical_not(last))
+        def _():
+            go_right(z, k).start()
+
+        @pl.when(jnp.logical_not(first))
+        def _():
+            go_left(z, k).start()
+
+        if k < CHUNKS:
+            go_y(z, k).start()
 
     tail_y().wait_recv()
 
@@ -144,31 +151,39 @@
 
     def arrivals(d):
         a, b = z - d, z + d
+        for k in range(CHUNKS + 1):
+            @pl.when(a >= 0)
+            def _():
+                go_right(a, k).wait_recv()
+
+                @pl.when(jnp.logical_not(last))
+                def _():
+                    go_right(a, k).start()
+
+                if k < CHUNKS:
+                    go_y(a, k).start()
+
+            @pl.when(b < nz)
+            def _():
+                go_left(b, k).wait_recv()
+
+                @pl.when(jnp.logical_not(first))
+                def _():
+                    go_left(b, k).start()
+
+                if k < CHUNKS:
+                    go_y(b, k).start()
 
         @pl.when(a >= 0)
         def _():
-            go_right(a).wait_recv()
+            tail_right(a).wait_recv()
 
             @pl.when(jnp.logical_not(last))
             def _():
-                go_right(a).start()
-
-            go_y(a).start()
-            tail_right(a).wait_recv()
-
-            @pl.when(jnp.logical_not(last))
-            def _():
                 tail_right(a).start()
 
         @pl.when(b < nz)
         def _():
-            go_left(b).wait_recv()
-
-            @pl.when(jnp.logical_not(first))
-            def _():
-                go_left(b).start()
-
-            go_y(b).start()
             tail_left(b).wait_recv()
 
             @pl.when(jnp.logical_not(first))
@@ -180,7 +195,8 @@
         return jnp.where(j % 2 == 1, z - d, z + d)
 
     def hidden(b):
-        go_y(b).wait_recv()
+        for k in range(CHUNKS):
+            go_y(b, k).wait_recv()
         packed = X[pl.ds(2 * b, 2), :, D:].reshape(2 * MAIN, CH)
         for q in range(PACK):
             pick = one_hot(16, 2 * MAIN, lambda r, c: (r < 2 * REST) & (c == (r // REST) * MAIN + REST * q + r % REST))
@@ -219,17 +235,20 @@
     lax.fori_loop(0, 2 * nz - 1, gather_step, 0)
     loads[2].wait()
 
-    def give_y(b):
-        return pltpu.make_async_remote_copy(
-            pb.at[2 * b + 1 - y, :, :cut], yr.at[b], sYr.at[b], rYr.at[b], device_id={"tp": partner})
-
-    def give_right(b):
-        return pltpu.make_async_remote_copy(
-            pb.at[2 * b + y], zr.at[b + 1], sZ.at[b], rL.at[b], device_id={"tp": t + 2})
-
-    def give_left(b):
-        return pltpu.make_async_remote_copy(
-            pb.at[2 * b + y], zr.at[b], sZ.at[b], rR.at[b], device_id={"tp": t - 2})
+    def give_y(b, k):
+        return pltpu.make_async_remote_copy(
+            pb.at[2 * b + 1 - y, :, span(k)], yr.at[b, :, span(k)], sYr.at[b, k], rYr.at[b, k],
+            device_id={"tp": partner})
+
+    def give_right(b, k):
+        return pltpu.make_async_remote_copy(
+            pb.at[2 * b + y, :, span(k)], zr.at[b + 1, :, span(k)], sZ.at[b, k], rL.at[b, k],
+            device_id={"tp": t + 2})
+
+    def give_left(b, k):
+        return pltpu.make_async_remote_copy(
+            pb.at[2 * b + y, :, span(k)], zr.at[b, :, span(k)], sZ.at[b, k], rR.at[b, k],
+            device_id={"tp": t - 2})
 
     def tail_give_right(b):
         return pltpu.make_async_remote_copy(
@@ -268,8 +287,10 @@
             pb[pl.ds(2 * b, 2), :, cols] = part[:2 * MAIN].reshape(2, MAIN, CH)
             put = one_hot(2 * MAIN, 16, lambda r, c: (c < 2 * REST) & (r == (c // REST) * MAIN + REST * q + c % REST))
             rest = rest + mm(put, part[2 * MAIN:])
+            for k in range(CHUNKS):
+                if q * CH < (k + 1) * step <= (q + 1) * CH:
+                    give_y(b, k).start()
         pb[pl.ds(2 * b, 2), :, D:] = rest.astype(BF16).reshape(2, MAIN, CH)
-        give_y(b).start()
 
     def add_in(i, start, stop, terms):
         for c in range(start, stop, 384):
@@ -322,42 +343,44 @@
         def _():
             tail_give_y().start()
 
-        give_y(b).wait_recv()
-
-        @pl.when(from_left)
-        def _():
-            give_right(b).wait_recv()
-
-        @pl.when(from_right)
-        def _():
-            give_left(b).wait_recv()
-
-        @pl.when(none)
-        def _():
-            add_in(mine, 0, cut, ((yr, b, 0),))
-
-        @pl.when(only_left)
-        def _():
-            add_in(mine, 0, cut, ((yr, b, 0), (zr, b + 1, 0)))
-            add_in(mine, cut, wide, ((zr, b + 1, 0),))
-
-        @pl.when(only_right)
-        def _():
-            add_in(mine, 0, cut, ((yr, b, 0), (zr, b, 0)))
-            add_in(mine, cut, wide, ((zr, b, 0),))
-
-        @pl.when(both)
-        def _():
-            add_in(mine, 0, cut, ((yr, b, 0), (zr, b + 1, 0), (zr, b, 0)))
-            add_in(mine, cut, wide, ((zr, b + 1, 0), (zr, b, 0)))
-
-        @pl.when(b > z)
-        def _():
-            give_right(b).start()
-
-        @pl.when(b < z)
-        def _():
-            give_left(b).start()
+        for k in (CHUNKS,) + tuple(range(CHUNKS)):
+            at, end = span(k).start, span(k).stop
+            own = ((yr, b, 0),) if k < CHUNKS else ()
+            if k < CHUNKS:
+                give_y(b, k).wait_recv()
+
+            @pl.when(from_left)
+            def _():
+                give_right(b, k).wait_recv()
+
+            @pl.when(from_right)
+            def _():
+                give_left(b, k).wait_recv()
+
+            if k < CHUNKS:
+                @pl.when(none)
+                def _():
+                    add_in(mine, at, end, own)
+
+            @pl.when(only_left)
+            def _():
+                add_in(mine, at, end, own + ((zr, b + 1, 0),))
+
+            @pl.when(only_right)
+            def _():
+                add_in(mine, at, end, own + ((zr, b, 0),))
+
+            @pl.when(both)
+            def _():
+                add_in(mine, at, end, own + ((zr, b + 1, 0), (zr, b, 0)))
+
+            @pl.when(b > z)
+            def _():
+                give_right(b, k).start()
+
+            @pl.when(b < z)
+            def _():
+                give_left(b, k).start()
 
     steps, lag = 2 * nz - 1, 3
 
@@ -413,27 +436,32 @@
     tail_give_y().wait_send()
 
     def finish(b, _):
-        go_y(b).wait_send()
-        give_y(b).wait_send()
+        for k in range(CHUNKS):
+            go_y(b, k).wait_send()
+            give_y(b, k).wait_send()
 
         @pl.when((b <= z) & jnp.logical_not(last))
         def _():
-            go_right(b).wait_send()
+            for k in range(CHUNKS + 1):
+                go_right(b, k).wait_send()
             tail_right(b).wait_send()
 
         @pl.when((b >= z) & jnp.logical_not(first))
         def _():
-            go_left(b).wait_send()
+            for k in range(CHUNKS + 1):
+                go_left(b, k).wait_send()
             tail_left(b).wait_send()
 
         @pl.when(b > z)
         def _():
-            give_right(b).wait_send()
+            for k in range(CHUNKS + 1):
+                give_right(b, k).wait_send()
             tail_give_right(b).wait_send()
 
         @pl.when(b < z)
         def _():
-            give_left(b).wait_send()
+            for k in range(CHUNKS + 1):
+                give_left(b, k).wait_send()
             tail_give_left(b).wait_send()
 
         return 0
@@ -446,7 +474,8 @@
     D = tokens.shape[1]
     F = w_gate.shape[2]
     wide = D + D // PACK
-    cut = wide - wide // 128 // 6 * 128
+    lanes = wide // 128
+    cut = (lanes - lanes // 6) // CHUNKS * CHUNKS * 128
     vmem = pl.BlockSpec(memory_space=pltpu.VMEM)
     hbm = pl.BlockSpec(memory_space=pl.ANY)
     dma = pltpu.SemaphoreType.DMA
@@ -470,7 +499,7 @@
             pltpu.VMEM((MAIN, D // 2), BF16),
             pltpu.VMEM((16, D // PACK), BF16),
             dma((3,)),
-        ] + [dma((nz,))] * 16 + [dma((2,))] * 4,
+        ] + [dma((nz, CHUNKS + 1))] * 10 + [dma((nz,))] * 6 + [dma((2,))] * 4,
         compiler_params=pltpu.CompilerParams(
             collective_id=0, has_side_effects=True, vmem_limit_bytes=62 * 2**20
         ),

time: 103 us -> 98.6 us (0.957)
  Pallas kernels: 101 us -> 96.4 us
    pallas_call x1, Pallas kernels: 101 us -> 96.4 us  [shards(): pl.pallas_call(functools.partial(kernel, n, cut), out_shape=jax.ShapeDtyp...]
where the time goes in v3:
time: 98.6 us; the launch traced here: 98.4 us
  Pallas kernels  96.4 us (98%)
  local copies, waits for them, and re-layouts  2.06 us (2%)
    pallas_call x1, Pallas kernels, shards(): pl.pallas_call(functools.partial(kernel, n, cut), out_shape=jax.ShapeDtyp...  96.4 us
    unnamed x1, local copies, waits for them, and re-layouts  2.06 us

profile of v3, /device:TPU:1, one launch (start us, length us, event | category | flops | bytes accessed | tf_op | source)
XLA Modules:
  0.0 98.4 jit_solution(7376984158335111986)
XLA Ops:
  0.0 96.4 %shard_map.73 = bf16[128,3072]{1,0:T(8,128)(2,1)} custom-call(bf16[128,6144]{1,0:T(8,128)(2,1)} %tok.1, s32[2,128]{1,0:T(2,128)} %bitcast.2, f32[2,128]{1,0:T(2,128)} %bitcast.3, s32[1,1,288]{2,1,0:T(1,128)} %bits.1, bf16[1,6144,1024]{2,1,0:T(8,128)(2,1)} %wg_hbm.1, bf16[1,6144,1024]{2,1,0:T(8,128)(2,1)} %wu_hbm.1, bf16[1,1024,6144]{2,1,0:T(8,128)(2,1)} %wd_hbm.1), custom_call_target="tpu_custom_call" | custom-call | flops 10871635968 | bytes 37748736 | tf_op jit(solution)/shard_map/pallas_call | solution.py:482
  96.4 2.1 %copy.9 = bf16[128,3072]{1,0:T(8,128)(2,1)} copy(bf16[128,3072]{1,0:T(8,128)(2,1)} %shard_map.73) | data formatting | bytes 1572864

commit v4 on v3

--- a/solution.py
+++ b/solution.py
@@ -29,7 +29,7 @@
 
 def kernel(
     n, cut, tok, ids, wts, bits, wg_hbm, wu_hbm, wd_hbm, out,
-    wg, wu, wd, X, xl, h, pb, yr, zr, zt, yt, em, ex,
+    wg, wu, wd, X, xl, ga, ua, h, pb, yr, zr, zt, yt, em, ex,
     wsem, sR, sL, sY, rz, ry, sYr, rYr, sZ, rL, rR, sRt, sLt, rzt, sZt, rLt, rRt, st, rt, se, re,
 ):
     nz = n // 2
@@ -83,6 +83,52 @@
         here = (c >= REST * q) & (c < REST * q + REST)
         return jnp.where(here & (row[:, :width] - MAIN == c - REST * q), 1.0, 0.0).astype(BF16)
 
+    neighbours = 4 - first.astype(jnp.int32) - last.astype(jnp.int32)
+    pl.semaphore_wait(barrier, neighbours)
+
+    step = cut // CHUNKS
+
+    def span(k):
+        return slice(k * step, (k + 1) * step) if k < CHUNKS else slice(cut, X.shape[2])
+
+    def go_right(b, k):
+        ref = X.at[2 * b + y, :, span(k)]
+        return pltpu.make_async_remote_copy(ref, ref, sR.at[b, k], rz.at[b, k], device_id={"tp": t + 2})
+
+    def go_left(b, k):
+        ref = X.at[2 * b + y, :, span(k)]
+        return pltpu.make_async_remote_copy(ref, ref, sL.at[b, k], rz.at[b, k], device_id={"tp": t - 2})
+
+    def go_y(b, k):
+        ref = X.at[2 * b + y, :, span(k)]
+        return pltpu.make_async_remote_copy(ref, ref, sY.at[b, k], ry.at[b, k], device_id={"tp": partner})
+
+    def tail_y():
+        return pltpu.make_async_remote_copy(
+            X.at[t, :, cut:], X.at[t, :, cut:], st.at[0], rt.at[0], device_id={"tp": partner})
+
+    def tail_right(b):
+        i = 2 * b + 1 - y
+        return pltpu.make_async_remote_copy(
+            X.at[i, :, cut:], X.at[i, :, cut:], sRt.at[b], rzt.at[b], device_id={"tp": t + 2})
+
+    def tail_left(b):
+        i = 2 * b + 1 - y
+        return pltpu.make_async_remote_copy(
+            X.at[i, :, cut:], X.at[i, :, cut:], sLt.at[b], rzt.at[b], device_id={"tp": t - 2})
+
+    def send_own(k):
+        @pl.when(jnp.logical_not(last))
+        def _():
+            go_right(z, k).start()
+
+        @pl.when(jnp.logical_not(first))
+        def _():
+            go_left(z, k).start()
+
+        if k < CHUNKS:
+            go_y(z, k).start()
+
     _, row = routing(e)
     hot = main_hot(row)
     rest = jnp.zeros((MAIN, CH), F32)
@@ -90,55 +136,12 @@
         part = tok[:, q * CH:(q + 1) * CH]
         X[t, :, q * CH:(q + 1) * CH] = mm(hot, part, ((0,), (0,))).astype(BF16)
         rest = rest + mm(rest_hot(row, q, MAIN), part, ((0,), (0,)))
+        for k in range(CHUNKS):
+            if q * CH < (k + 1) * step <= (q + 1) * CH:
+                send_own(k)
     X[t, :, D:] = rest.astype(BF16)
-
-    neighbours = 4 - first.astype(jnp.int32) - last.astype(jnp.int32)
-    pl.semaphore_wait(barrier, neighbours)
-
-    step = cut // CHUNKS
-
-    def span(k):
-        return slice(k * step, (k + 1) * step) if k < CHUNKS else slice(cut, X.shape[2])
-
-    def go_right(b, k):
-        ref = X.at[2 * b + y, :, span(k)]
-        return pltpu.make_async_remote_copy(ref, ref, sR.at[b, k], rz.at[b, k], device_id={"tp": t + 2})
-
-    def go_left(b, k):
-        ref = X.at[2 * b + y, :, span(k)]
-        return pltpu.make_async_remote_copy(ref, ref, sL.at[b, k], rz.at[b, k], device_id={"tp": t - 2})
-
-    def go_y(b, k):
-        ref = X.at[2 * b + y, :, span(k)]
-        return pltpu.make_async_remote_copy(ref, ref, sY.at[b, k], ry.at[b, k], device_id={"tp": partner})
-
-    def tail_y():
-        return pltpu.make_async_remote_copy(
-            X.at[t, :, cut:], X.at[t, :, cut:], st.at[0], rt.at[0], device_id={"tp": partner})
-
-    def tail_right(b):
-        i = 2 * b + 1 - y
-        return pltpu.make_async_remote_copy(
-            X.at[i, :, cut:], X.at[i, :, cut:], sRt.at[b], rzt.at[b], device_id={"tp": t + 2})
-
-    def tail_left(b):
-        i = 2 * b + 1 - y
-        return pltpu.make_async_remote_copy(
-            X.at[i, :, cut:], X.at[i, :, cut:], sLt.at[b], rzt.at[b], device_id={"tp": t - 2})
-
     tail_y().start()
-    for k in range(CHUNKS + 1):
-        @pl.when(jnp.logical_not(last))
-        def _():
-            go_right(z, k).start()
-
-        @pl.when(jnp.logical_not(first))
-        def _():
-            go_left(z, k).start()
-
-        if k < CHUNKS:
-            go_y(z, k).start()
-
+    send_own(CHUNKS)
     tail_y().wait_recv()
 
     @pl.when(jnp.logical_not(last))
@@ -195,23 +198,31 @@
         return jnp.where(j % 2 == 1, z - d, z + d)
 
     def hidden(b):
-        for k in range(CHUNKS):
-            go_y(b, k).wait_recv()
         packed = X[pl.ds(2 * b, 2), :, D:].reshape(2 * MAIN, CH)
         for q in range(PACK):
             pick = one_hot(16, 2 * MAIN, lambda r, c: (r < 2 * REST) & (c == (r // REST) * MAIN + REST * q + r % REST))
-            cols = slice(q * CH, (q + 1) * CH)
-            xl[:2 * MAIN, cols] = X[pl.ds(2 * b, 2), :, cols].reshape(2 * MAIN, CH)
-            xl[2 * MAIN:, cols] = mm(pick, packed).astype(BF16)
-
-        def tile(i, _):
-            cols = pl.ds(pl.multiple_of(i * 256, 256), 256)
-            g = mm(xl[...], wg[:, cols])
-            u = mm(xl[...], wu[:, cols])
-            h[b, :, cols] = ((g / (1.0 + jnp.exp(-g))) * u).astype(BF16)
-            return 0
-
-        lax.fori_loop(0, F // 256, tile, 0)
+            xl[2 * MAIN:, q * CH:(q + 1) * CH] = mm(pick, packed).astype(BF16)
+
+        for k in range(CHUNKS):
+            deep = slice(k * step, (k + 1) * step if k < CHUNKS - 1 else D)
+            go_y(b, k).wait_recv()
+            xl[:2 * MAIN, deep] = X[pl.ds(2 * b, 2), :, deep].reshape(2 * MAIN, deep.stop - deep.start)
+
+            def tile(i, _):
+                cols = pl.ds(pl.multiple_of(i * 256, 256), 256)
+                g = mm(xl[:, deep], wg[deep, cols])
+                u = mm(xl[:, deep], wu[deep, cols])
+                if k > 0:
+                    g = g + ga[:, cols]
+                    u = u + ua[:, cols]
+                if k < CHUNKS - 1:
+                    ga[:, cols] = g
+                    ua[:, cols] = u
+                else:
+                    h[b, :, cols] = ((g / (1.0 + jnp.exp(-g))) * u).astype(BF16)
+                return 0
+
+            lax.fori_loop(0, F // 256, tile, 0)
 
     arrivals(1)
     loads[0].wait()
@@ -490,6 +501,8 @@
             pltpu.VMEM((F, D), BF16),
             pltpu.VMEM((n, MAIN, wide), BF16),
             pltpu.VMEM((PAIR, D), BF16),
+            pltpu.VMEM((PAIR, F), F32),
+            pltpu.VMEM((PAIR, F), F32),
             pltpu.VMEM((nz, PAIR, F), BF16),
             pltpu.VMEM((n, MAIN, wide), BF16),
             pltpu.VMEM((nz, MAIN, cut), BF16),

time: 98.6 us -> 102 us (1.034)
  Pallas kernels: 96.4 us -> 99.3 us
    pallas_call x1, Pallas kernels: 96.4 us -> 99.3 us  [shards(): pl.pallas_call(functools.partial(kernel, n, cut), out_shape=jax.ShapeDtyp...]
where the time goes in v4:
time: 102 us; the launch traced here: 101 us
  Pallas kernels  99.3 us (97%)
  local copies, waits for them, and re-layouts  2.06 us (2%)
    pallas_call x1, Pallas kernels, shards(): pl.pallas_call(functools.partial(kernel, n, cut), out_shape=jax.ShapeDtyp...  99.3 us
    unnamed x1, local copies, waits for them, and re-layouts  2.06 us

profile of v4, /device:TPU:1, one launch (start us, length us, event | category | flops | bytes accessed | tf_op | source)
XLA Modules:
  0.0 101.4 jit_solution(15267683484059305375)
XLA Ops:
  0.0 99.3 %shard_map.73 = bf16[128,3072]{1,0:T(8,128)(2,1)} custom-call(bf16[128,6144]{1,0:T(8,128)(2,1)} %tok.1, s32[2,128]{1,0:T(2,128)} %bitcast.2, f32[2,128]{1,0:T(2,128)} %bitcast.3, s32[1,1,288]{2,1,0:T(1,128)} %bits.1, bf16[1,6144,1024]{2,1,0:T(8,128)(2,1)} %wg_hbm.1, bf16[1,6144,1024]{2,1,0:T(8,128)(2,1)} %wu_hbm.1, bf16[1,1024,6144]{2,1,0:T(8,128)(2,1)} %wd_hbm.1), custom_call_target="tpu_custom_call" | custom-call | flops 10871635968 | bytes 37748736 | tf_op jit(solution)/shard_map/pallas_call | solution.py:493
  99.3 2.1 %copy.9 = bf16[128,3072]{1,0:T(8,128)(2,1)} copy(bf16[128,3072]{1,0:T(8,128)(2,1)} %shard_map.73) | data formatting | bytes 1572864

commit v5 on v3

--- a/solution.py
+++ b/solution.py
@@ -11,7 +11,7 @@
 MAIN = 32
 REST = SLOT - MAIN
 PACK = MAIN // REST
-CHUNKS = 3
+CHUNKS = 5
 PAIR = 2 * MAIN + 16
 F32 = jnp.float32
 BF16 = jnp.bfloat16

time: 98.6 us -> 99.7 us (1.011)
  Pallas kernels: 96.4 us -> 97.4 us
    pallas_call x1, Pallas kernels: 96.4 us -> 97.4 us  [shards(): pl.pallas_call(functools.partial(kernel, n, cut), out_shape=jax.ShapeDtyp...]
where the time goes in v5:
time: 99.7 us; the launch traced here: 99.5 us
  Pallas kernels  97.4 us (98%)
  local copies, waits for them, and re-layouts  2.06 us (2%)
    pallas_call x1, Pallas kernels, shards(): pl.pallas_call(functools.partial(kernel, n, cut), out_shape=jax.ShapeDtyp...  97.4 us
    unnamed x1, local copies, waits for them, and re-layouts  2.06 us

profile of v5, /device:TPU:1, one launch (start us, length us, event | category | flops | bytes accessed | tf_op | source)
XLA Modules:
  0.0 99.5 jit_solution(13523272883257591281)
XLA Ops:
  0.0 97.4 %shard_map.73 = bf16[128,3072]{1,0:T(8,128)(2,1)} custom-call(bf16[128,6144]{1,0:T(8,128)(2,1)} %tok.1, s32[2,128]{1,0:T(2,128)} %bitcast.2, f32[2,128]{1,0:T(2,128)} %bitcast.3, s32[1,1,288]{2,1,0:T(1,128)} %bits.1, bf16[1,6144,1024]{2,1,0:T(8,128)(2,1)} %wg_hbm.1, bf16[1,6144,1024]{2,1,0:T(8,128)(2,1)} %wu_hbm.1, bf16[1,1024,6144]{2,1,0:T(8,128)(2,1)} %wd_hbm.1), custom_call_target="tpu_custom_call" | custom-call | flops 10871635968 | bytes 37748736 | tf_op jit(solution)/shard_map/pallas_call | solution.py:482
  97.4 2.1 %copy.9 = bf16[128,3072]{1,0:T(8,128)(2,1)} copy(bf16[128,3072]{1,0:T(8,128)(2,1)} %shard_map.73) | data formatting | bytes 1572864
